TPU v7x, 32 devices: a whole 2x2x4 slice. The times are simulated.
32 devices in a mesh: replica: 4 (over y, core), expert: 4 (over z), dp: 2 (over x).
Axes of the slice: x: 2, y: 2, z: 4, core: 2. Of those that a mesh axis runs over, the one named last changes fastest.
Arguments:
- tokens: bfloat16 [4, 1024, 3072], P('replica', ('expert', 'dp')), may hold values from -6 to 6
- routes: int32 [4, 1024, 2], P('replica', ('expert', 'dp')), may hold values from 0 to 3, all different within a row; in each aligned block of 128 rows (0 to 127, 128 to 255, ..., all dimensions but the last counted through in order) at most 96 rows name the same one
- route_weight: float32 [4, 1024, 2], P('replica', ('expert', 'dp')), may hold values from 0.1 to 1
- cotangent: bfloat16 [4, 1024, 3072], P('replica', ('expert', 'dp')), may hold values from -6 to 6
- gate_weight: bfloat16 [4, 4, 3072, 512], P('replica', 'expert', None, 'dp'), may hold values from -0.109375 to 0.109375
- up_weight: bfloat16 [4, 4, 3072, 512], P('replica', 'expert', None, 'dp'), may hold values from -0.109375 to 0.109375
- down_weight: bfloat16 [4, 4, 512, 3072], P('replica', 'expert', 'dp'), may hold values from -0.25 to 0.25
- pseudo_grad: float32 [4, 4, 512, 3072], P('replica', 'expert', 'dp'), may hold values from -6 to 6
- anchor: float32 [4, 512, 3072], P('expert', 'dp', 'replica'), may hold values from -6 to 6
- momentum: float32 [4, 512, 3072], P('expert', 'dp', 'replica'), may hold values from -3 to 3
Outputs:
- layer_out: bfloat16 [4, 1024, 3072], P('replica', ('expert', 'dp'))
- mix_grad: float32 [4, 1024, 2], P('replica', ('expert', 'dp'))
- token_grad: bfloat16 [4, 1024, 3072], P('replica', ('expert', 'dp'))
- gate_grad: bfloat16 [4, 4, 3072, 512], P('replica', 'expert', None, 'dp')
- up_grad: bfloat16 [4, 4, 3072, 512], P('replica', 'expert', None, 'dp')
- down_grad: bfloat16 [4, 4, 512, 3072], P('replica', 'expert', 'dp')
- new_anchor: float32 [4, 512, 3072], P('expert', 'dp', 'replica')
- new_momentum: float32 [4, 512, 3072], P('expert', 'dp', 'replica')
Inputs may be any that keep to these rules, and one draw needn't show every extreme that they name: `routes`: within the 128 rows of one block no expert is named by more than 96 of the rows, a bound that some block reaches.
All inputs are finite; a program needn't handle non-finite values.
Results may differ from a plain program's by a relative error of at most 0.0072.
Values may be sent and summed in bfloat16 or wider, within the bound.
A program may use at most 192 MiB of HBM per device.

v0:
```python
import jax
import jax.numpy as jnp
from jax import lax
from jax.sharding import PartitionSpec as P

OUTER_MU = 0.9
OUTER_RATE = 0.7


def rounded(value):
    return lax.optimization_barrier(value.astype(jnp.bfloat16)).astype(jnp.float32)


def destinations(choice_ids, experts, capacity):
    flat_ids = choice_ids.reshape(-1)
    onehot = (flat_ids[:, None] == jnp.arange(experts, dtype=jnp.int32)[None, :]).astype(jnp.int32)
    counts = jnp.cumsum(onehot, axis=0)
    rank_slot = jnp.sum(counts * onehot, axis=1) - 1
    return (flat_ids * capacity + rank_slot).reshape(choice_ids.shape)


def silu_parts(gate_pre):
    sigmoid_gate = jax.nn.sigmoid(gate_pre)
    return (gate_pre * sigmoid_gate, sigmoid_gate * (1.0 + gate_pre * (1.0 - sigmoid_gate)))


def group_sum(left, right, form):
    parts = jnp.einsum(form, left, right, preferred_element_type=jnp.float32)
    return jnp.sum(rounded(parts), axis=0).astype(jnp.bfloat16)


def contract_last(left, right):
    return lax.dot_general(
        left, right, (((1,), (1,)), ((), ())), preferred_element_type=jnp.float32
    )


def expert_slab(rows_in, rows_cot, gate_w, up_w, down_w, group_form, down_form):
    width = rows_in.shape[-1]
    lead_dims = rows_in.shape[:-1]
    flat_in = rows_in.reshape(-1, width)
    flat_cot = rows_cot.reshape(-1, width)
    gate_pre = jnp.dot(flat_in, gate_w, preferred_element_type=jnp.float32)
    up_pre = jnp.dot(flat_in, up_w, preferred_element_type=jnp.float32)
    silu_gate, silu_slope = silu_parts(gate_pre)
    hidden = (silu_gate * up_pre).astype(jnp.bfloat16)
    y_part = jnp.dot(hidden, down_w, preferred_element_type=jnp.float32)
    back_hidden = contract_last(flat_cot, down_w)
    gate_delta = (back_hidden * up_pre * silu_slope).astype(jnp.bfloat16)
    up_delta = (back_hidden * silu_gate).astype(jnp.bfloat16)
    dx_part = contract_last(gate_delta, gate_w) + contract_last(up_delta, up_w)
    slab_width = gate_w.shape[1]
    gate_grad = group_sum(rows_in, gate_delta.reshape(lead_dims + (slab_width,)), group_form)
    up_grad = group_sum(rows_in, up_delta.reshape(lead_dims + (slab_width,)), group_form)
    down_grad = group_sum(hidden.reshape(lead_dims + (slab_width,)), rows_cot, down_form)
    return (y_part, dx_part, gate_grad, up_grad, down_grad)


def shards(
    tokens,
    routes,
    route_weight,
    cotangent,
    gate_weight,
    up_weight,
    down_weight,
    pseudo_grad,
    anchor,
    momentum,
):
    island_count = lax.axis_size("replica")
    grad_local = pseudo_grad[0, 0]
    summed = lax.psum_scatter(
        grad_local.astype(jnp.bfloat16), "replica", scatter_dimension=1, tiled=True
    ).astype(jnp.float32)
    mean_grad = summed / island_count
    new_momentum = OUTER_MU * momentum[0] + mean_grad
    new_anchor = anchor[0] - OUTER_RATE * (mean_grad + OUTER_MU * new_momentum)
    experts = lax.axis_size("expert")
    slabs = lax.axis_size("dp")
    tok_rows = tokens[0]
    cot_rows = cotangent[0]
    choice_ids = routes[0]
    mix_weight = route_weight[0]
    tok_count, per_token = choice_ids.shape
    width = tok_rows.shape[1]
    capacity = min(tok_count, 3 * tok_count * per_token // (2 * experts))
    slot_dest = destinations(choice_ids, experts, capacity)
    targets = jnp.arange(experts * capacity, dtype=jnp.int32)
    matches = targets[:, None, None] == slot_dest[None, :, :]
    picker = jnp.any(matches, axis=2).astype(jnp.bfloat16)
    slot_weight = jnp.sum(jnp.where(matches, mix_weight[None], 0.0), axis=(1, 2))
    send_in = jnp.dot(picker, tok_rows, preferred_element_type=jnp.float32).astype(jnp.bfloat16)
    send_in = send_in.reshape(experts, capacity, width)
    send_cot = (
        jnp.dot(picker, cot_rows, preferred_element_type=jnp.float32) * slot_weight[:, None]
    ).astype(jnp.bfloat16)
    send_cot = send_cot.reshape(experts, capacity, width)
    gate_w = gate_weight[0, 0]
    up_w = up_weight[0, 0]
    down_w = down_weight[0, 0]
    fan_in = jnp.broadcast_to(send_in[:, None], (experts, slabs, capacity, width)).reshape(
        experts * slabs, capacity, width
    )
    fan_cot = jnp.broadcast_to(send_cot[:, None], (experts, slabs, capacity, width)).reshape(
        experts * slabs, capacity, width
    )
    got_in, got_cot = (
        lax.all_to_all(fan_in, ("expert", "dp"), split_axis=0, concat_axis=0, tiled=True),
        lax.all_to_all(fan_cot, ("expert", "dp"), split_axis=0, concat_axis=0, tiled=True),
    )
    got_in = got_in.reshape(experts, slabs, capacity, width)
    got_cot = got_cot.reshape(experts, slabs, capacity, width)
    y_part, dx_part, gate_grad, up_grad, down_grad = expert_slab(
        got_in, got_cot, gate_w, up_w, down_w, "abmd,abmf->bdf", "abmf,abmd->bfd"
    )
    back_y = y_part.astype(jnp.bfloat16).reshape(experts * slabs, capacity, width)
    back_dx = dx_part.astype(jnp.bfloat16).reshape(experts * slabs, capacity, width)
    ret_y, ret_dx = (
        lax.all_to_all(back_y, ("expert", "dp"), split_axis=0, concat_axis=0, tiled=True),
        lax.all_to_all(back_dx, ("expert", "dp"), split_axis=0, concat_axis=0, tiled=True),
    )
    expert_out = jnp.sum(
        ret_y.reshape(experts, slabs, capacity, width).astype(jnp.float32), axis=1
    ).astype(jnp.bfloat16)
    expert_dx = jnp.sum(
        ret_dx.reshape(experts, slabs, capacity, width).astype(jnp.float32), axis=1
    ).astype(jnp.bfloat16)
    out_flat = expert_out.reshape(experts * capacity, width)
    dx_flat = expert_dx.reshape(experts * capacity, width)
    picked = (
        jnp.take(out_flat, slot_dest.reshape(-1), axis=0)
        .reshape(tok_count, per_token, width)
        .astype(jnp.float32)
    )
    picked_dx = (
        jnp.take(dx_flat, slot_dest.reshape(-1), axis=0)
        .reshape(tok_count, per_token, width)
        .astype(jnp.float32)
    )
    layer_out = jnp.sum(picked * mix_weight[:, :, None], axis=1).astype(jnp.bfloat16)
    mix_grad = jnp.sum(picked * cot_rows[:, None, :].astype(jnp.float32), axis=2)
    token_grad = jnp.sum(picked_dx, axis=1).astype(jnp.bfloat16)
    return (
        layer_out[None],
        mix_grad[None],
        token_grad[None],
        gate_grad[None, None],
        up_grad[None, None],
        down_grad[None, None],
        new_anchor[None],
        new_momentum[None],
    )


def solution(mesh):
    return jax.shard_map(
        shards,
        mesh=mesh,
        in_specs=(
            P("replica", ("expert", "dp"), None),
            P("replica", ("expert", "dp"), None),
            P("replica", ("expert", "dp"), None),
            P("replica", ("expert", "dp"), None),
            P("replica", "expert", None, "dp"),
            P("replica", "expert", None, "dp"),
            P("replica", "expert", "dp", None),
            P("replica", "expert", "dp", None),
            P("expert", "dp", "replica"),
            P("expert", "dp", "replica"),
        ),
        out_specs=(
            P("replica", ("expert", "dp"), None),
            P("replica", ("expert", "dp"), None),
            P("replica", ("expert", "dp"), None),
            P("replica", "expert", None, "dp"),
            P("replica", "expert", None, "dp"),
            P("replica", "expert", "dp", None),
            P("expert", "dp", "replica"),
            P("expert", "dp", "replica"),
        ),
        check_vma=False,
    )
```

profile of v0, /device:TPU:0, one launch (start us, length us, event | category | flops | bytes accessed | tf_op | source)
XLA Modules:
  0.0 502.4 jit_solution(2425392183434676823)
XLA Ops:
  7.2 0.9 copy.50
  8.2 0.1 eq.45
  8.4 1.2 reduce-window.6
  10.2 0.7 add_bitcast_fusion.1
  11.0 1.9 convolution_convert_fusion.1
  12.9 2.8 broadcast_in_dim.61
  15.7 7.4 %all-to-all-start = ((bf16[8,96,3072]{2,1,0:T(8,128)(2,1)}), bf16[8,96,3072]{2,1,0:T(8,128)(2,1)}, u32[]{:S(2)}, u32[]{:S(2)}) async-start(bf16[8,96,3072]{2,1,0:T(8,128)(2,1)} %bitcast.107), calls=%async_computation | async-start | bytes 9437184 | tf_op jit(solution)/shard_map/all_to_all | solution.py:109
  23.0 0.1 select_reduce_fusion
  23.2 2.2 multiply_convert_fusion
  25.4 102.2 %all-to-all-done = bf16[8,96,3072]{2,1,0:T(8,128)(2,1)} async-done(((bf16[8,96,3072]{2,1,0:T(8,128)(2,1)}), bf16[8,96,3072]{2,1,0:T(8,128)(2,1)}, u32[]{:S(2)}, u32[]{:S(2)}) %all-to-all-start) | async-done | bytes 4718624 | tf_op jit(solution)/shard_map/all_to_all | solution.py:109
  127.6 4.4 broadcast_in_dim.66
  132.0 4.6 all-to-all-start.2
  136.6 5.2 %fusion.4 = f32[768,256]{1,0:T(8,128)} fusion(bf16[768,3072]{1,0:T(8,128)(2,1)} %bitcast.6, bf16[1,1,3072,256]{3,2,1,0:T(8,128)(2,1)} %param.17), kind=kOutput, calls=%fused_computation.17 | convolution fusion | flops 1207959552 | bytes 7077888 | tf_op jit(solution)/shard_map/dot_general | solution.py:44
  141.8 4.6 fusion.8
  146.4 93.9 %all-to-all-done.2 = bf16[8,96,3072]{2,1,0:T(8,128)(2,1)} async-done(((bf16[8,96,3072]{2,1,0:T(8,128)(2,1)}), bf16[8,96,3072]{2,1,0:T(8,128)(2,1)}, u32[]{:S(2)}, u32[]{:S(2)}) %all-to-all-start.2) | async-done | bytes 4718624 | tf_op jit(solution)/shard_map/all_to_all | solution.py:110
  240.3 5.3 %multiply_convert_fusion.1 = (bf16[768,256]{1,0:T(8,128)(2,1)}, bf16[768,256]{1,0:T(8,128)(2,1)}, bf16[768,256]{1,0:T(8,128)(2,1)S(1)}) fusion(f32[768,256]{1,0:T(8,128)} %fusion.8, f32[768,256]{1,0:T(8,128)} %fusion.4, bf16[768,3072]{1,0:T(8,128)(2,1)} %bitcast.18, bf16[1,1,256,3072]{3,2,1,0:T(8,128)(2,1)S(1)} %copy-done), kind=kOutput, calls=%fused_computation.33 | convolution fusion | flops 1210908672 | bytes 9043968 | tf_op jit(solution)/shard_map/dot_general | solution.py:33
  245.6 3.6 convolution_convert_fusion
  249.2 4.7 all-to-all-start.1
  254.0 1.4 fusion.6
  255.4 3.6 add_convert_fusion
  259.0 98.7 %all-to-all-done.1 = bf16[8,96,3072]{2,1,0:T(8,128)(2,1)} async-done(((bf16[8,96,3072]{2,1,0:T(8,128)(2,1)}), bf16[8,96,3072]{2,1,0:T(8,128)(2,1)}, u32[]{:S(2)}, u32[]{:S(2)}) %all-to-all-start.1) | async-done | bytes 4718624 | tf_op jit(solution)/shard_map/all_to_all | solution.py:120
  357.7 4.8 all-to-all-start.3
  362.6 10.4 %reduce-scatter.2.cloned.1.call-start = ((), (), s32[]{:S(2)}) async-start(), calls=%async_computation.5 | async-start | bytes 1966080 | tf_op jit(solution)/shard_map/reduce_scatter | solution.py:73
  373.0 1.4 convert_bitcast_fusion
  374.4 0.7 copy.55
  375.1 1.3 bitcast_convert_fusion.3
  376.4 1.1 mul.89
  377.5 3.4 mul.90
  380.9 22.8 %reduce-scatter.2.cloned.1.call-done = bf16[256,768]{1,0:T(8,128)(2,1)} async-done(((bf16[256,3072]{1,0:T(8,128)(2,1)}), bf16[256,768]{1,0:T(8,128)(2,1)}) %reduce-scatter.2.cloned.1.call-update) | async-done | bytes 393232 | tf_op jit(solution)/shard_map/reduce_scatter | solution.py:73
  403.8 2.8 fusion.14
  406.6 4.2 bitcast_convert_fusion
  410.8 6.2 %bitcast_convert_fusion.1 = bf16[2,3072,256]{2,1,0:T(8,128)(2,1)} fusion(bf16[4,2,96,3072]{3,2,1,0:T(8,128)(2,1)} %bitcast.23, bf16[4,2,96,256]{3,2,1,0:T(8,128)(2,1)S(1)} %bitcast.119), kind=kOutput, calls=%fused_computation.4 | convolution fusion | flops 1209532416 | bytes 8257536 | tf_op jit(solution)/shard_map/abmd,abmf->bdf/dot_general | solution.py:28
  417.0 2.2 reduce_sum.117
  419.2 4.1 reduce_sum.116
  423.3 4.5 bitcast_convert_fusion.2
  427.8 2.2 reduce_sum.115
  429.9 3.6 bitcast_reduce_fusion.1
  433.6 2.7 gather_fusion
  436.3 3.1 multiply_reduce_fusion
  439.5 0.6 copy.56
  440.2 26.1 %all-to-all-done.3 = bf16[8,96,3072]{2,1,0:T(8,128)(2,1)} async-done(((bf16[8,96,3072]{2,1,0:T(8,128)(2,1)}), bf16[8,96,3072]{2,1,0:T(8,128)(2,1)}, u32[]{:S(2)}, u32[]{:S(2)}) %all-to-all-start.3) | async-done | bytes 4718624 | tf_op jit(solution)/shard_map/all_to_all | solution.py:121
  466.3 3.7 bitcast_reduce_fusion
  470.0 2.7 gather_fusion.1
  472.7 3.9 broadcast_select_fusion
  476.6 0.6 reshape.129
  477.2 5.1 %reduce_sum.114 = bf16[128,3072]{1,0:T(8,128)(2,1)} reduce(bf16[128,2,3072]{2,1,0:T(2,128)(2,1)S(1)} %reshape.129, bf16[]{:T(256)} %constant.36.clone.1), dimensions={1}, to_apply=%region_9.11 | reduce | flops 393216 | bytes 2359298 | tf_op jit(solution)/shard_map/reduce_sum | solution.py:143
  482.3 5.4 %reshape.135 = f32[128,2,3072]{2,1,0:T(2,128)} reshape(f32[256,3072]{1,0:T(8,128)} %get-tuple-element.41) | data formatting | bytes 6291456 | tf_op jit(solution)/shard_map/convert_element_type | solution.py:134
  487.8 7.3 %multiply_reduce_fusion.1 = bf16[128,3072]{1,0:T(8,128)(2,1)} fusion(f32[128,2,3072]{2,1,0:T(2,128)} %reshape.135, f32[128,2]{1,0:T(8,128)S(1)} %copy-done.10), kind=kLoop, calls=%fused_computation.12 | loop fusion | flops 1179648 | bytes 3933184 | tf_op jit(solution)/shard_map/reduce_sum | solution.py:141
  (41 shorter events, 1.0 us)
Async XLA Ops:
  7.2 233.2 %copy-start = (bf16[1,1,256,3072]{3,2,1,0:T(8,128)(2,1)S(1)}, bf16[1,1,256,3072]{3,2,1,0:T(8,128)(2,1)}, u32[]{:S(2)}) copy-start(bf16[1,1,256,3072]{3,2,1,0:T(8,128)(2,1)} %param.18) | copy-start | bytes 4718596
  15.6 7.4 %copy-start.11 = (f32[1,128,2]{1,2,0:T(2,128)S(1)}, f32[1,128,2]{1,2,0:T(2,128)}, u32[]{:S(2)}) copy-start(f32[1,128,2]{1,2,0:T(2,128)} %param.14) | copy-start | bytes 3076
  15.6 7.5 %copy-start.3 = (bf16[1,128,3072]{2,1,0:T(8,128)(2,1)S(1)}, bf16[1,128,3072]{2,1,0:T(8,128)(2,1)}, u32[]{:S(2)}) copy-start(bf16[1,128,3072]{2,1,0:T(8,128)(2,1)} %param.15) | copy-start | bytes 2359300
  15.7 111.9 %all-to-all-start = ((bf16[8,96,3072]{2,1,0:T(8,128)(2,1)}), bf16[8,96,3072]{2,1,0:T(8,128)(2,1)}, u32[]{:S(2)}, u32[]{:S(2)}) async-start(bf16[8,96,3072]{2,1,0:T(8,128)(2,1)} %bitcast.107), calls=%async_computation | async-start | bytes 9437184 | tf_op jit(solution)/shard_map/all_to_all | solution.py:109
  132.0 108.3 %all-to-all-start.2 = ((bf16[8,96,3072]{2,1,0:T(8,128)(2,1)}), bf16[8,96,3072]{2,1,0:T(8,128)(2,1)}, u32[]{:S(2)}, u32[]{:S(2)}) async-start(bf16[8,96,3072]{2,1,0:T(8,128)(2,1)} %bitcast.108), calls=%async_computation.2 | async-start | bytes 9437184 | tf_op jit(solution)/shard_map/all_to_all | solution.py:110
  136.6 5.2 %copy-start.4 = (bf16[1,1,3072,256]{3,2,1,0:T(8,128)(2,1)S(1)}, bf16[1,1,3072,256]{3,2,1,0:T(8,128)(2,1)}, u32[]{:S(2)}) copy-start(bf16[1,1,3072,256]{3,2,1,0:T(8,128)(2,1)} %param.16) | copy-start | bytes 4718596
  249.2 4.7 copy-start.6
  249.2 108.5 %all-to-all-start.1 = ((bf16[8,96,3072]{2,1,0:T(8,128)(2,1)}), bf16[8,96,3072]{2,1,0:T(8,128)(2,1)}, u32[]{:S(2)}, u32[]{:S(2)}) async-start(bf16[8,96,3072]{2,1,0:T(8,128)(2,1)} %bitcast.106), calls=%async_computation.1 | async-start | bytes 9437184 | tf_op jit(solution)/shard_map/all_to_all | solution.py:120
  253.9 1.5 copy-start.5
  254.0 1.5 copy-start.8
  357.7 15.3 %copy-start.2 = (f32[1,1,256,3072]{3,2,1,0:T(8,128)S(1)}, f32[1,1,256,3072]{3,2,1,0:T(8,128)}, u32[]{:S(2)}) copy-start(f32[1,1,256,3072]{3,2,1,0:T(8,128)} %param.19) | copy-start | bytes 9437188
  357.7 108.6 %all-to-all-start.3 = ((bf16[8,96,3072]{2,1,0:T(8,128)(2,1)}), bf16[8,96,3072]{2,1,0:T(8,128)(2,1)}, u32[]{:S(2)}, u32[]{:S(2)}) async-start(bf16[8,96,3072]{2,1,0:T(8,128)(2,1)} %bitcast.109), calls=%async_computation.3 | async-start | bytes 9437184 | tf_op jit(solution)/shard_map/all_to_all | solution.py:121
  362.6 41.2 %reduce-scatter.2.cloned.1.call-start = ((), (), s32[]{:S(2)}) async-start(), calls=%async_computation.5 | async-start | bytes 1966080 | tf_op jit(solution)/shard_map/reduce_scatter | solution.py:73
  406.6 4.2 copy-start.9
  419.2 4.1 copy-start.7
  482.3 5.5 %copy-start.10 = (f32[128,2]{1,0:T(8,128)S(1)}, f32[128,2]{1,0:T(8,128)}, u32[]{:S(2)}) copy-start(f32[128,2]{1,0:T(8,128)} %copy.55) | copy-start | bytes 3076
  482.3 12.7 %copy-start.1 = (bf16[1,1,256,3072]{3,2,1,0:T(8,128)(2,1)S(1)}, bf16[1,1,256,3072]{3,2,1,0:T(8,128)(2,1)}, u32[]{:S(2)}) copy-start(bf16[1,1,256,3072]{3,2,1,0:T(8,128)(2,1)} %param.18) | copy-start | bytes 4718596
Sparse Core Ops, SparseCore 0:
  374.5 29.2 reduce-scatter.1
where the time goes:
time: 511 us; the launch traced here: 502 us
  waiting for transfers between devices  344 us (67%)
  other arithmetic  42.9 us (8%)
  matrix products  42.7 us (8%)
  starting transfers between devices  32 us (6%)
  local copies, waits for them, and re-layouts  26.4 us (5%)
  between operations  14.7 us (3%)
    all_to_all x1, waiting for transfers between devices, shards(): lax.all_to_all(fan_in, ('expert', 'dp'), split_axis=0, concat_axis=0, til...  102 us
    all_to_all x1, waiting for transfers between devices, shards(): lax.all_to_all(back_y, ('expert', 'dp'), split_axis=0, concat_axis=0, til...  98.7 us
    all_to_all x1, waiting for transfers between devices, shards(): lax.all_to_all(fan_cot, ('expert', 'dp'), split_axis=0, concat_axis=0, ti...  93.9 us
    all_to_all x1, waiting for transfers between devices, shards(): lax.all_to_all(back_dx, ('expert', 'dp'), split_axis=0, concat_axis=0, ti...  26.1 us
    reduce_scatter x1, waiting for transfers between devices, shards(): lax.psum_scatter(grad_local.astype(jnp.bfloat16), 'replica', scatter_dime...  22.8 us
    dot_general x3, matrix products, group_sum(): parts = jnp.einsum(form, left, right, preferred_element_type=jnp.float32)  14.9 us
    reduce_scatter x1, starting transfers between devices, shards(): lax.psum_scatter(grad_local.astype(jnp.bfloat16), 'replica', scatter_dime...  10.4 us
    dot_general x3, matrix products, contract_last(): lax.dot_general(left, right, (((1,), (1,)), ((), ())), preferred_element_...  10.3 us
  transfers between devices with their start and end apart: 5, of which 5 were waited for; matrix products, arithmetic and copies ran while one was open for 12% of the time, Pallas kernels for 0%

commit v1 on v0

v1 whole, which is shorter than its diff:
```python
import functools

import jax
import jax.numpy as jnp
from jax import lax
from jax.experimental import pallas as pl
from jax.experimental.pallas import tpu as pltpu
from jax.sharding import PartitionSpec as P

OUTER_MU = 0.9
OUTER_RATE = 0.7


def contract_last(left, right):
    return lax.dot_general(
        left, right, (((1,), (1,)), ((), ())), preferred_element_type=jnp.float32
    )


def contract_first(left, right):
    return lax.dot_general(
        left, right, (((0,), (0,)), ((), ())), preferred_element_type=jnp.float32
    )


MESH = pl.DeviceIdType.MESH
VMEM_BYTES = 58 * 2**20
CHUNK = 16


def enter(levels):
    e, x = lax.axis_index("expert"), lax.axis_index("dp")
    barrier = pltpu.get_barrier_semaphore()
    pl.semaphore_signal(barrier, inc=1, device_id={"dp": 1 - x}, device_id_type=MESH)

    @pl.when(e > 0)
    def _():
        pl.semaphore_signal(barrier, inc=1, device_id={"expert": e - 1}, device_id_type=MESH)

    @pl.when(e < levels - 1)
    def _():
        pl.semaphore_signal(barrier, inc=1, device_id={"expert": e + 1}, device_id_type=MESH)

    at_end = (e == 0) | (e == levels - 1)

    @pl.when(at_end)
    def _():
        pl.semaphore_wait(barrier, 2)

    @pl.when(jnp.logical_not(at_end))
    def _():
        pl.semaphore_wait(barrier, 3)


def remote(src, dst, sems, device):
    return pltpu.make_async_remote_copy(
        src_ref=src, dst_ref=dst, send_sem=sems[0], recv_sem=sems[1], device_id=device, device_id_type=MESH
    )


def gather_kernel(levels, tok, cot, tok_all, cot_all, own_sem, z_send, z_recv, x_send, x_recv, ex_send, ex_recv):
    e, x = lax.axis_index("expert"), lax.axis_index("dp")
    last = levels - 1
    mine, full = (tok, cot), (tok_all, cot_all)
    pos = (e, last - e)
    sign = (-1, 1)
    enter(levels)
    local = [pltpu.make_async_copy(mine[a], full[a].at[e, x], own_sem.at[a]) for a in range(2)]
    for copy in local:
        copy.start()

    def z_copy(d, k, a):
        level = e + sign[d] * (k - 1)
        src = mine[a] if k == 1 else full[a].at[level, x]
        return remote(src, full[a].at[level, x], (z_send.at[d, k, a], z_recv.at[d, k, a]), {"expert": e - sign[d]})

    def z_in(d, k, a):
        level = e + sign[d] * k
        ref = full[a].at[level, x]
        return remote(ref, ref, (z_send.at[d, k, a], z_recv.at[d, k, a]), {"expert": e + sign[d]})

    def x_copy(d, k, a):
        level = e + sign[d] * k
        src = mine[a] if k == 0 else full[a].at[level, x]
        return remote(src, full[a].at[level, x], (x_send.at[d, k, a], x_recv.at[d, k, a]), {"dp": 1 - x})

    def x_in(d, k, a):
        ref = full[a].at[e + sign[d] * k, 1 - x]
        return remote(ref, ref, (x_send.at[d, k, a], x_recv.at[d, k, a]), {"dp": 1 - x})

    def ex_copy(d, go):
        ref = cot_all.at[0 if d == 0 else last, 1 - x]
        return remote(ref, ref, (ex_send.at[d], ex_recv.at[d]), {"expert": e - sign[d] if go else e + sign[d]})

    def crosses(d, k, a):
        return pos[d] > k if a == 1 else pos[d] >= k

    for a in range(2):
        x_copy(0, 0, a).start()
        for d in range(2):
            @pl.when(pos[d] < last)
            def _(d=d, a=a):
                z_copy(d, 1, a).start()

    for k in range(1, levels):
        for a in range(2):
            for d in range(2):
                @pl.when(pos[d] >= k)
                def _(d=d, k=k, a=a):
                    z_in(d, k, a).wait_recv()

                    if k < last:
                        @pl.when(pos[d] < last)
                        def _():
                            z_copy(d, k + 1, a).start()

                @pl.when(crosses(d, k, a))
                def _(d=d, k=k, a=a):
                    x_copy(d, k, a).start()

        if k == 1:
            x_in(0, 0, 1).wait_recv()
            for d in range(2):
                @pl.when(pos[d] == 0)
                def _(d=d):
                    ex_copy(d, True).start()

        for d in range(2):
            @pl.when(pos[d] == k)
            def _(d=d):
                ex_copy(d, False).wait_recv()

                @pl.when(pos[d] < last)
                def _():
                    ex_copy(d, True).start()

    x_in(0, 0, 0).wait_recv()
    for a in range(2):
        x_copy(0, 0, a).wait_send()
    for k in range(1, levels):
        for a in range(2):
            for d in range(2):
                @pl.when(crosses(d, k, a))
                def _(d=d, k=k, a=a):
                    x_in(d, k, a).wait_recv()
                    x_copy(d, k, a).wait_send()

                @pl.when((pos[d] < last) & (pos[d] >= k - 1))
                def _(d=d, k=k, a=a):
                    z_copy(d, k, a).wait_send()

    for d in range(2):
        @pl.when(pos[d] < last)
        def _(d=d):
            ex_copy(d, True).wait_send()
    for copy in local:
        copy.wait()


def scatter_kernel(
    levels, y, dx, y_out, dx_out, held, zbuf, ex, z_send, z_recv, x_send, x_recv, ex_send, ex_recv
):
    e, x = lax.axis_index("expert"), lax.axis_index("dp")
    last = levels - 1
    part, outs = (y, dx), (y_out, dx_out)
    pos = (e, last - e)
    sign = (-1, 1)
    rows = y.shape[2]
    enter(levels)

    def add(dst, srcs):
        def body(i, carry):
            at = pl.ds(pl.multiple_of(i * CHUNK, CHUNK), CHUNK)
            total = srcs[0][at, :].astype(jnp.float32)
            for src in srcs[1:]:
                total = total + src[at, :].astype(jnp.float32)
            dst[at, :] = total.astype(dst.dtype)
            return carry

        lax.fori_loop(0, rows // CHUNK, body, 0)

    def owner(d, k):
        return e + sign[d] * k

    def x_copy(d, k, a, src=None):
        s = owner(d, k)
        src = part[a].at[s, 1 - x] if src is None else src
        return remote(src, held.at[a, s], (x_send.at[d, k, a], x_recv.at[d, k, a]), {"dp": 1 - x})

    def z_copy(d, k, a):
        s = owner(d, k)
        return remote(held.at[a, s], zbuf.at[d, a, s], (z_send.at[d, k, a], z_recv.at[d, k, a]), {"expert": e + sign[d]})

    def z_in(d, k, a):
        ref = zbuf.at[d, a, owner(d, k)]
        return remote(ref, ref, (z_send.at[d, k + 1, a], z_recv.at[d, k + 1, a]), {"expert": e - sign[d]})

    def ex_copy(d):
        end = 0 if d == 0 else last
        return remote(ex.at[d], ex.at[2 + d], (ex_send.at[d], ex_recv.at[d]), {"expert": e + sign[d]})

    def crosses(d, k, a):
        return pos[d] > k if a == 1 else pos[d] >= k

    at_end = (e == 0) | (e == last)

    for d in range(2):
        end = 0 if d == 0 else last

        @pl.when(pos[d] == last)
        def _(d=d, end=end):
            add(ex.at[d], [dx.at[end, 1 - x]])
            ex_copy(d).start()

    for k in range(last, 0, -1):
        for a in range(2):
            for d in range(2):
                @pl.when(crosses(d, k, a))
                def _(d=d, k=k, a=a):
                    x_copy(d, k, a).start()
    x_copy(0, 0, 0).start()

    @pl.when(jnp.logical_not(at_end))
    def _():
        x_copy(0, 0, 1).start()

    for k in range(last, 0, -1):
        for a in (1, 0):
            for d in range(2):
                @pl.when(pos[d] >= k)
                def _(d=d, k=k, a=a):
                    s = owner(d, k)
                    own = part[a].at[s, x]
                    slot = held.at[a, s]

                    def ready(crossed):
                        if k < last:
                            @pl.when(pos[d] < last)
                            def _():
                                z_in(d, k, a).wait_recv()
                                add(slot, [own, zbuf.at[d, a, s]] + ([slot] if crossed else []))

                        @pl.when(pos[d] == last)
                        def _():
                            add(slot, [own] + ([slot] if crossed else []))

                    if a == 0:
                        x_copy(d, k, a).wait_recv()
                        ready(True)
                    else:
                        @pl.when(pos[d] > k)
                        def _():
                            x_copy(d, k, a).wait_recv()
                            ready(True)

                        @pl.when(pos[d] == k)
                        def _():
                            ready(False)
                    z_copy(d, k, a).start()

        for d in range(2):
            end = 0 if d == 0 else last

            @pl.when(pos[d] == k - 1)
            def _(d=d, end=end, k=k):
                ex_copy(d).wait_recv()
                add(ex.at[d], [ex.at[2 + d], dx.at[end, 1 - x]])
                if k > 1:
                    ex_copy(d).start()
                else:
                    x_copy(0, 0, 1, ex.at[d]).start()

    for a in range(2):
        x_copy(0, 0, a).wait_recv()
        near = [part[a].at[e, x], held.at[a, e]]

        @pl.when(e < last)
        def _(a=a):
            z_in(0, 0, a).wait_recv()

        @pl.when(e > 0)
        def _(a=a):
            z_in(1, 0, a).wait_recv()

        @pl.when(e == 0)
        def _(a=a, near=near):
            add(outs[a], near + [zbuf.at[0, a, e]])

        @pl.when(e == last)
        def _(a=a, near=near):
            add(outs[a], near + [zbuf.at[1, a, e]])

        @pl.when(jnp.logical_not(at_end))
        def _(a=a, near=near):
            add(outs[a], near + [zbuf.at[0, a, e], zbuf.at[1, a, e]])

    for a in range(2):
        x_copy(0, 0, a).wait_send()
        for k in range(1, levels):
            for d in range(2):
                @pl.when(crosses(d, k, a))
                def _(d=d, k=k, a=a):
                    x_copy(d, k, a).wait_send()

                @pl.when(pos[d] >= k)
                def _(d=d, k=k, a=a):
                    z_copy(d, k, a).wait_send()

    for d in range(2):
        @pl.when(pos[d] > 0)
        def _(d=d):
            ex_copy(d).wait_send()


def sems(levels):
    shape = (2, levels + 1, 2)
    return [pltpu.SemaphoreType.DMA(shape)] * 4 + [pltpu.SemaphoreType.DMA((2,))] * 2


def gather_rows(tok, cot, levels, lines):
    if not by_kernel(tok.shape, levels, lines):
        return tuple(lax.all_gather(v, ("expert", "dp"), axis=0, tiled=True) for v in (tok, cot))
    full = jax.ShapeDtypeStruct((levels, lines) + tok.shape, tok.dtype)
    got = pl.pallas_call(
        functools.partial(gather_kernel, levels),
        out_shape=(full, full),
        in_specs=[pl.BlockSpec(memory_space=pl.ANY)] * 2,
        out_specs=(pl.BlockSpec(memory_space=pl.ANY),) * 2,
        scratch_shapes=[pltpu.SemaphoreType.DMA((2,))] + sems(levels),
        compiler_params=pltpu.CompilerParams(collective_id=0, has_side_effects=True),
    )(tok, cot)
    return tuple(v.reshape(-1, tok.shape[1]) for v in got)


def scatter_sums(y_part, dx_part, levels, lines):
    width = y_part.shape[1]
    rows = y_part.shape[0] // (levels * lines)
    if not by_kernel((rows, width), levels, lines):
        return tuple(
            lax.psum_scatter(v, ("expert", "dp"), scatter_dimension=0, tiled=True) for v in (y_part, dx_part)
        )
    one = jax.ShapeDtypeStruct((rows, width), y_part.dtype)
    vmem = pl.BlockSpec(memory_space=pltpu.VMEM)
    return pl.pallas_call(
        functools.partial(scatter_kernel, levels),
        out_shape=(one, one),
        in_specs=[vmem] * 2,
        out_specs=(vmem,) * 2,
        scratch_shapes=[
            pltpu.VMEM((2, levels, rows, width), y_part.dtype),
            pltpu.VMEM((2, 2, levels, rows, width), y_part.dtype),
            pltpu.VMEM((4, rows, width), y_part.dtype),
        ]
        + sems(levels),
        compiler_params=pltpu.CompilerParams(
            collective_id=1, has_side_effects=True, vmem_limit_bytes=VMEM_BYTES
        ),
    )(
        y_part.reshape(levels, lines, rows, width), dx_part.reshape(levels, lines, rows, width)
    )


def by_kernel(block, levels, lines):
    rows, width = block
    blocks = 2 * levels * lines + 6 * levels + 6
    return lines == 2 and levels > 2 and rows % CHUNK == 0 and 2 * blocks * rows * width < VMEM_BYTES


def shards(
    tokens,
    routes,
    route_weight,
    cotangent,
    gate_weight,
    up_weight,
    down_weight,
    pseudo_grad,
    anchor,
    momentum,
):
    axes = ("expert", "dp")
    me = lax.axis_index("expert")
    levels, lines = lax.axis_size("expert"), lax.axis_size("dp")
    tok, cot = gather_rows(tokens[0], cotangent[0], levels, lines)
    ids = lax.all_gather(routes[0].T, axes, axis=1, tiled=True)
    wts = lax.all_gather(route_weight[0].T, axes, axis=1, tiled=True)
    hit = ids == me
    weight = jnp.sum(jnp.where(hit, wts, 0.0), axis=0)[:, None]
    gate_w = gate_weight[0, 0]
    up_w = up_weight[0, 0]
    down_w = down_weight[0, 0]

    gate_pre = jnp.dot(tok, gate_w, preferred_element_type=jnp.float32)
    up_pre = jnp.dot(tok, up_w, preferred_element_type=jnp.float32)
    sig = jax.nn.sigmoid(gate_pre)
    silu_gate = gate_pre * sig
    hidden = silu_gate * up_pre
    hidden_w = (hidden * weight).astype(jnp.bfloat16)
    y_part = jnp.dot(hidden_w, down_w, preferred_element_type=jnp.float32).astype(jnp.bfloat16)

    back = contract_last(cot, down_w)
    mix_rows = jnp.sum(hidden * back, axis=1)
    back_w = back * weight
    gate_delta = (back_w * up_pre * (sig * (1.0 + gate_pre * (1.0 - sig)))).astype(jnp.bfloat16)
    up_delta = (back_w * silu_gate).astype(jnp.bfloat16)
    dx_part = (contract_last(gate_delta, gate_w) + contract_last(up_delta, up_w)).astype(jnp.bfloat16)
    layer_out, token_grad = scatter_sums(y_part, dx_part, levels, lines)
    mix_part = jnp.where(hit, mix_rows[None, :], 0.0)
    mix_grad = lax.psum_scatter(mix_part, axes, scatter_dimension=1, tiled=True).T

    gate_grad = contract_first(tok, gate_delta).astype(jnp.bfloat16)
    up_grad = contract_first(tok, up_delta).astype(jnp.bfloat16)
    down_grad = contract_first(hidden_w, cot).astype(jnp.bfloat16)

    island_count = lax.axis_size("replica")
    summed = lax.psum_scatter(
        pseudo_grad[0, 0].astype(jnp.bfloat16), "replica", scatter_dimension=1, tiled=True
    ).astype(jnp.float32)
    mean_grad = summed / island_count
    new_momentum = OUTER_MU * momentum[0] + mean_grad
    new_anchor = anchor[0] - OUTER_RATE * (mean_grad + OUTER_MU * new_momentum)
    return (
        layer_out[None],
        mix_grad[None],
        token_grad[None],
        gate_grad[None, None],
        up_grad[None, None],
        down_grad[None, None],
        new_anchor[None],
        new_momentum[None],
    )


ROWS = P("replica", ("expert", "dp"), None)
COLS = P("replica", "expert", None, "dp")
HIDS = P("replica", "expert", "dp", None)
OUTER = P("expert", "dp", "replica")


def solution(mesh):
    return jax.shard_map(
        shards,
        mesh=mesh,
        in_specs=(ROWS, ROWS, ROWS, ROWS, COLS, COLS, HIDS, HIDS, OUTER, OUTER),
        out_specs=(ROWS, ROWS, ROWS, COLS, COLS, HIDS, OUTER, OUTER),
        check_vma=False,
    )
```

time: 511 us -> 342 us (0.67); the launches traced: 502 us -> 341 us
  waiting for transfers between devices: 344 us -> 0.04 us
  Pallas kernels: 0 us -> 237 us
  blocking collectives: 0 us -> 39.3 us
  other arithmetic: 42.9 us -> 5.79 us
  starting transfers between devices: 32 us -> 0.26 us
  local copies, waits for them, and re-layouts: 26.4 us -> 4.76 us
    all_to_all x4 -> x0, waiting for transfers between devices: 321 us -> none  [the longest x1 102 us: shards(): lax.all_to_all(fan_in, ('expert', 'dp'), split_axis=0, concat_axis=0, til...]
    pallas_call x0 -> x2, Pallas kernels: none -> 237 us  [the longest x1 122 us: scatter_sums(): pl.pallas_call(functools.partial(scatter_kernel, levels), out_shape=(one,...]
    all_gather x0 -> x2, blocking collectives: none -> 39.3 us  [the longest x1 22.6 us: shards(): ids = lax.all_gather(routes[0].T, axes, axis=1, tiled=True)]
    reduce_sum x10 -> x1, other arithmetic: 31.4 us -> 0.02 us  [shards(): weight = jnp.sum(jnp.where(hit, wts, 0.0), axis=0)[:, None]]
    reduce_scatter x1, waiting for transfers between devices: 22.8 us -> 0.01 us  [shards(): lax.psum_scatter(pseudo_grad[0, 0].astype(jnp.bfloat16), 'replica', scatt...]
    all_to_all x4 -> x0, starting transfers between devices: 21.5 us -> none  [the longest x1 7.38 us: shards(): lax.all_to_all(fan_in, ('expert', 'dp'), split_axis=0, concat_axis=0, til...]
    reduce_scatter x1, starting transfers between devices: 10.4 us -> 0.22 us  [shards(): lax.psum_scatter(pseudo_grad[0, 0].astype(jnp.bfloat16), 'replica', scatt...]
    broadcast_in_dim x3 -> x0, local copies, waits for them, and re-layouts: 7.31 us -> none  [the longest x1 4.42 us: shards(): jnp.broadcast_to(send_cot[:, None], (experts, slabs, capacity, width))]
  transfers between devices with their start and end apart: 5 -> 2, of which waited for: 5 -> 0; matrix products, arithmetic and copies ran while one was open for 12% -> 10% of each run, Pallas kernels for 0% -> 36%
where the time goes in v1:
time: 342 us; the launch traced here: 341 us
  Pallas kernels  237 us (69%)
  matrix products  39.9 us (12%)
  blocking collectives  39.3 us (11%)
  between operations  14.2 us (4%)
  other arithmetic  5.79 us (2%)
  local copies, waits for them, and re-layouts  4.76 us (1%)
    pallas_call x1, Pallas kernels, scatter_sums(): pl.pallas_call(functools.partial(scatter_kernel, levels), out_shape=(one,...  122 us
    pallas_call x1, Pallas kernels, gather_rows(): pl.pallas_call(functools.partial(gather_kernel, levels), out_shape=(full,...  114 us
    all_gather x1, blocking collectives, shards(): ids = lax.all_gather(routes[0].T, axes, axis=1, tiled=True)  22.6 us
    dot_general x3, matrix products, contract_first(): lax.dot_general(left, right, (((0,), (0,)), ((), ())), preferred_element_...  17.5 us
    all_gather x1, blocking collectives, shards(): wts = lax.all_gather(route_weight[0].T, axes, axis=1, tiled=True)  16.7 us
    dot_general x3, matrix products, contract_last(): lax.dot_general(left, right, (((1,), (1,)), ((), ())), preferred_element_...  9.83 us
  transfers between devices with their start and end apart: 2, of which 0 were waited for; matrix products, arithmetic and copies ran while one was open for 10% of the time, Pallas kernels for 36%

profile of v1, /device:TPU:0, one launch (start us, length us, event | category | flops | bytes accessed | tf_op | source)
XLA Modules:
  0.0 340.8 jit_solution(518965618232192802)
XLA Ops:
  7.2 0.0 copy-start
  7.2 0.0 reduce-scatter.7.cloned.1.call-start
  7.2 22.6 %all_gather.6 = s32[2,1024]{1,0:T(2,128)S(1)} all-gather(s32[2,128]{1,0:T(2,128)} %bitcast.79), channel_id=1, replica_groups=mesh['replica'=4,'expert'=4,'dp'=2] {'expert','dp'}, dimensions={1}, use_global_device_ids=true | all-gather | bytes 9216 | tf_op jit(solution)/shard_map/all_gather | solution.py:385
  29.9 16.7 %all_gather.7 = f32[2,1024]{1,0:T(2,128)S(1)} all-gather(f32[2,128]{1,0:T(2,128)} %bitcast.80), channel_id=1, replica_groups=mesh['replica'=4,'expert'=4,'dp'=2] {'expert','dp'}, dimensions={1}, use_global_device_ids=true | all-gather | bytes 9216 | tf_op jit(solution)/shard_map/all_gather | solution.py:386
  46.5 114.3 %shard_map.161 = (bf16[4,2,128,3072]{3,2,1,0:T(8,128)(2,1)}, bf16[4,2,128,3072]{3,2,1,0:T(8,128)(2,1)}) custom-call(bf16[128,3072]{1,0:T(8,128)(2,1)} %bitcast.73, bf16[128,3072]{1,0:T(8,128)(2,1)} %bitcast.74), custom_call_target="tpu_custom_call" | custom-call | tf_op jit(solution)/shard_map/pallas_call | solution.py:324
  160.8 0.0 copy-start.1
  160.8 0.0 copy-start.10
  160.8 0.0 slice-start
  160.8 5.2 %fusion.7 = f32[1024,256]{0,1:T(8,128)S(1)} fusion(bf16[1024,3072]{1,0:T(8,128)(2,1)} %bitcast.81, bf16[1,1,3072,256]{3,2,1,0:T(8,128)(2,1)} %param.15), kind=kOutput, calls=%fused_computation.12 | convolution fusion | flops 1610612736 | bytes 8912896 | tf_op jit(solution)/shard_map/dot_general | solution.py:394
  166.0 0.0 copy-done.1
  166.0 0.3 copy-done.10
  166.3 0.0 slice-start.1
  166.3 1.9 fusion.11
  168.2 0.0 copy-done
  168.3 0.0 slice-done
  168.3 0.2 slice-done.1
  168.4 3.4 %multiply_reduce_fusion = (f32[1024]{0:T(1024)S(1)}, bf16[1024,256]{0,1:T(8,128)(2,1)}, bf16[1024,256]{0,1:T(8,128)(2,1)}, bf16[1024,256]{0,1:T(8,128)(2,1)}) fusion(f32[1024,256]{0,1:T(8,128)S(1)} %fusion.7, f32[1024,256]{0,1:T(8,128)S(1)} %fusion.11, f32[1024]{0:T(1024)S(1)} %select_reduce_fusion, bf16[1024,3072]{1,0:T(8,128)(2,1)S(1)} %bitcast.88, ...), kind=kOutput, calls=%fused_computation.19 | convolution fusion | flops 1615592448 | bytes 11542528 | tf_op jit(solution)/shard_map/dot_general | solution.py:15
  171.9 1.0 copy.18
  172.9 0.0 reduce-scatter.7.cloned.1.call-update
  172.9 0.2 reduce-scatter.5.cloned.1.call-start
  173.2 3.3 convert_bitcast_fusion
  176.5 0.0 reduce-scatter.5.cloned.1.call-update
  176.5 0.0 copy-start.9
  176.5 5.5 %convolution_convert_fusion = bf16[1024,3072]{1,0:T(8,128)(2,1)} fusion(bf16[1024,256]{0,1:T(8,128)(2,1)} %get-tuple-element.18, bf16[1,1,256,3072]{3,2,1,0:T(8,128)(2,1)S(1)} %copy-done), kind=kOutput, calls=%fused_computation.1 | convolution fusion | flops 1613758464 | bytes 8388608 | tf_op jit(solution)/shard_map/dot_general | solution.py:399
  182.0 0.0 copy-done.9
  182.0 0.0 copy-start.2
  182.0 0.0 copy-start.8
  182.0 1.9 fusion.9
  183.9 0.0 copy-done.2
  183.9 0.0 copy-done.8
  183.9 4.5 %add_convert_fusion = bf16[1024,3072]{1,0:T(8,128)(2,1)} fusion(f32[1024,3072]{1,0:T(8,128)S(1)} %fusion.9, bf16[1024,256]{0,1:T(8,128)(2,1)S(1)} %copy-done.8, bf16[1,1,3072,256]{3,2,1,0:T(8,128)(2,1)S(1)} %copy-done.2), kind=kOutput, calls=%fused_computation | convolution fusion | flops 1616904192 | bytes 20971520 | tf_op jit(solution)/shard_map/dot_general | solution.py:15
  188.4 0.0 copy-start.3
  188.4 122.3 %shard_map.162 = (bf16[128,3072]{1,0:T(8,128)(2,1)}, bf16[128,3072]{1,0:T(8,128)(2,1)}) custom-call(bf16[4,2,128,3072]{3,2,1,0:T(8,128)(2,1)} %bitcast.70, bf16[4,2,128,3072]{3,2,1,0:T(8,128)(2,1)} %bitcast.71), custom_call_target="tpu_custom_call" | custom-call | tf_op jit(solution)/shard_map/pallas_call | solution.py:344
  310.8 0.0 copy-done.3
  310.8 5.7 %fusion.2 = bf16[1,1,256,3072]{3,2,1,0:T(8,128)(2,1)} fusion(bf16[1024,256]{0,1:T(8,128)(2,1)S(1)} %copy-done.3, bf16[1024,3072]{1,0:T(8,128)(2,1)} %bitcast.85), kind=kOutput, calls=%fused_computation.7 | convolution fusion | flops 1611399168 | bytes 8388608 | tf_op jit(solution)/shard_map/dot_general | solution.py:21
  316.5 5.8 %fusion = bf16[1,1,3072,256]{3,2,1,0:T(8,128)(2,1)} fusion(bf16[1024,3072]{1,0:T(8,128)(2,1)} %bitcast.82, bf16[1024,256]{0,1:T(8,128)(2,1)S(1)} %copy-done.9), kind=kOutput, calls=%fused_computation.5 | convolution fusion | flops 1611399168 | bytes 8388608 | tf_op jit(solution)/shard_map/dot_general | solution.py:21
  322.3 0.0 copy-start.4
  322.3 0.0 copy-start.5
  322.3 5.9 %fusion.1 = bf16[1,1,3072,256]{3,2,1,0:T(8,128)(2,1)} fusion(bf16[1024,3072]{1,0:T(8,128)(2,1)} %bitcast.83, bf16[1024,256]{0,1:T(8,128)(2,1)S(1)} %copy-done.8), kind=kOutput, calls=%fused_computation.6 | convolution fusion | flops 1611399168 | bytes 8388608 | tf_op jit(solution)/shard_map/dot_general | solution.py:21
  328.3 1.5 copy.19
  329.8 0.0 copy-done.4
  329.8 0.0 copy-done.5
  329.8 0.0 copy-start.6
  329.8 2.5 fusion.15
  332.2 0.0 copy-done.7
  332.2 0.9 copy.22
  333.1 0.0 copy-done.6
  333.1 0.9 copy.23
  (6 shorter events, 0.0 us)
Async XLA Ops:
  7.2 161.1 %copy-start = (bf16[1,1,256,3072]{3,2,1,0:T(8,128)(2,1)S(1)}, bf16[1,1,256,3072]{3,2,1,0:T(8,128)(2,1)}, u32[]{:S(2)}) copy-start(bf16[1,1,256,3072]{3,2,1,0:T(8,128)(2,1)} %param.16) | copy-start | bytes 4718596
  7.2 321.1 %reduce-scatter.7.cloned.1.call-start = ((), (), s32[]{:S(2)}) async-start(), calls=%async_computation.3 | async-start | bytes 589824
  160.8 5.2 %copy-start.1 = (bf16[1,1,3072,256]{3,2,1,0:T(8,128)(2,1)S(1)}, bf16[1,1,3072,256]{3,2,1,0:T(8,128)(2,1)}, u32[]{:S(2)}) copy-start(bf16[1,1,3072,256]{3,2,1,0:T(8,128)(2,1)} %param.14) | copy-start | bytes 4718596
  160.8 5.5 %copy-start.10 = (bf16[4,2,128,3072]{3,2,1,0:T(8,128)(2,1)S(1)}, bf16[4,2,128,3072]{3,2,1,0:T(8,128)(2,1)}, u32[]{:S(2)}) copy-start(bf16[4,2,128,3072]{3,2,1,0:T(8,128)(2,1)} %get-tuple-element.12) | copy-start | bytes 18874372
  160.8 7.4 %slice-start = ((s8[6291456]{0:T(1024)(128)(4,1)}), s8[4194304]{0:T(1024)(128)(4,1)S(1)}, s32[]{:S(2)}) async-start(s8[6291456]{0:T(1024)(128)(4,1)} %bitcast.86), calls=%async_computation.4 | async-start | bytes 8388608
  166.3 2.1 slice-start.1
  172.9 156.8 %reduce-scatter.5.cloned.1.call-start = ((), (), s32[]{:S(2)}) async-start(), calls=%async_computation.2 | async-start | bytes 1966080 | tf_op jit(solution)/shard_map/reduce_scatter | solution.py:416
  176.5 5.5 %copy-start.9 = (bf16[1024,256]{0,1:T(8,128)(2,1)S(1)}, bf16[1024,256]{0,1:T(8,128)(2,1)}, u32[]{:S(2)}) copy-start(bf16[1024,256]{0,1:T(8,128)(2,1)} %get-tuple-element.17) | copy-start | bytes 1572868
  182.0 1.9 copy-start.2
  182.0 1.9 copy-start.8
  188.4 122.3 %copy-start.3 = (bf16[1024,256]{0,1:T(8,128)(2,1)S(1)}, bf16[1024,256]{0,1:T(8,128)(2,1)}, u32[]{:S(2)}) copy-start(bf16[1024,256]{0,1:T(8,128)(2,1)} %get-tuple-element.18) | copy-start | bytes 1572868
  322.3 7.4 %copy-start.4 = (f32[1,256,768]{2,1,0:T(8,128)S(1)}, f32[1,256,768]{2,1,0:T(8,128)}, u32[]{:S(2)}) copy-start(f32[1,256,768]{2,1,0:T(8,128)} %param.19) | copy-start | bytes 2359300
  322.3 7.4 %copy-start.5 = (f32[1,256,768]{2,1,0:T(8,128)S(1)}, f32[1,256,768]{2,1,0:T(8,128)}, u32[]{:S(2)}) copy-start(f32[1,256,768]{2,1,0:T(8,128)} %param.18) | copy-start | bytes 2359300
  329.8 2.5 copy-start.7
  329.8 3.4 copy-start.6
Sparse Core Ops, SparseCore 0:
  173.0 61.7 reduce-scatter.6
  237.5 27.1 reduce-scatter.4

commit v2 on v1

--- a/solution.py
+++ b/solution.py
@@ -26,6 +26,7 @@
 MESH = pl.DeviceIdType.MESH
 VMEM_BYTES = 58 * 2**20
 CHUNK = 16
+TILE = 256
 
 
 def enter(levels):
@@ -58,14 +59,15 @@
     )
 
 
-def gather_kernel(levels, tok, cot, tok_all, cot_all, own_sem, z_send, z_recv, x_send, x_recv, ex_send, ex_recv):
+def gather_kernel(levels, tok, cot, meta, tok_all, cot_all, meta_all, own_sem, z_send, z_recv, x_send, x_recv, ex_send, ex_recv):
     e, x = lax.axis_index("expert"), lax.axis_index("dp")
     last = levels - 1
-    mine, full = (tok, cot), (tok_all, cot_all)
+    mine, full = (tok, cot, meta), (tok_all, cot_all, meta_all)
+    order = (2, 0, 1)
     pos = (e, last - e)
     sign = (-1, 1)
     enter(levels)
-    local = [pltpu.make_async_copy(mine[a], full[a].at[e, x], own_sem.at[a]) for a in range(2)]
+    local = [pltpu.make_async_copy(mine[a], full[a].at[e, x], own_sem.at[a]) for a in order]
     for copy in local:
         copy.start()
 
@@ -95,7 +97,7 @@
     def crosses(d, k, a):
         return pos[d] > k if a == 1 else pos[d] >= k
 
-    for a in range(2):
+    for a in order:
         x_copy(0, 0, a).start()
         for d in range(2):
             @pl.when(pos[d] < last)
@@ -103,7 +105,7 @@
                 z_copy(d, 1, a).start()
 
     for k in range(1, levels):
-        for a in range(2):
+        for a in order:
             for d in range(2):
                 @pl.when(pos[d] >= k)
                 def _(d=d, k=k, a=a):
@@ -135,10 +137,11 @@
                     ex_copy(d, True).start()
 
     x_in(0, 0, 0).wait_recv()
-    for a in range(2):
+    x_in(0, 0, 2).wait_recv()
+    for a in order:
         x_copy(0, 0, a).wait_send()
     for k in range(1, levels):
-        for a in range(2):
+        for a in order:
             for d in range(2):
                 @pl.when(crosses(d, k, a))
                 def _(d=d, k=k, a=a):
@@ -158,7 +161,35 @@
 
 
 def scatter_kernel(
-    levels, y, dx, y_out, dx_out, held, zbuf, ex, z_send, z_recv, x_send, x_recv, ex_send, ex_recv
+    levels,
+    y,
+    dx,
+    gate_delta,
+    up_delta,
+    hidden_w,
+    tok_hbm,
+    cot_hbm,
+    y_out,
+    dx_out,
+    gate_hbm,
+    up_hbm,
+    down_hbm,
+    held,
+    zbuf,
+    ex,
+    tok,
+    cot,
+    gate_grad,
+    up_grad,
+    down_grad,
+    load_sem,
+    store_sem,
+    z_send,
+    z_recv,
+    x_send,
+    x_recv,
+    ex_send,
+    ex_recv,
 ):
     e, x = lax.axis_index("expert"), lax.axis_index("dp")
     last = levels - 1
@@ -166,7 +197,25 @@
     pos = (e, last - e)
     sign = (-1, 1)
     rows = y.shape[2]
+    loads = [pltpu.make_async_copy(tok_hbm, tok, load_sem.at[0]), pltpu.make_async_copy(cot_hbm, cot, load_sem.at[1])]
+    for copy in loads:
+        copy.start()
     enter(levels)
+    tiles = tok.shape[1] // TILE
+    slots = 2 * last
+
+    def contract(left, right):
+        return contract_first(left, right).astype(jnp.bfloat16)
+
+    def gradients(slot):
+        def body(i, carry):
+            at = pl.ds(pl.multiple_of(i * TILE, TILE), TILE)
+            gate_grad[at, :] = contract(tok[:, at], gate_delta[...])
+            up_grad[at, :] = contract(tok[:, at], up_delta[...])
+            down_grad[:, at] = contract(hidden_w[...], cot[:, at])
+            return carry
+
+        lax.fori_loop(slot * tiles // slots, (slot + 1) * tiles // slots, body, 0)
 
     def add(dst, srcs):
         def body(i, carry):
@@ -224,8 +273,12 @@
     def _():
         x_copy(0, 0, 1).start()
 
+    for copy in loads:
+        copy.wait()
+
     for k in range(last, 0, -1):
         for a in (1, 0):
+            gradients(2 * (last - k) + 1 - a)
             for d in range(2):
                 @pl.when(pos[d] >= k)
                 def _(d=d, k=k, a=a):
@@ -270,6 +323,14 @@
                 else:
                     x_copy(0, 0, 1, ex.at[d]).start()
 
+    stores = [
+        pltpu.make_async_copy(gate_grad, gate_hbm, store_sem.at[0]),
+        pltpu.make_async_copy(up_grad, up_hbm, store_sem.at[1]),
+        pltpu.make_async_copy(down_grad, down_hbm, store_sem.at[2]),
+    ]
+    for copy in stores:
+        copy.start()
+
     for a in range(2):
         x_copy(0, 0, a).wait_recv()
         near = [part[a].at[e, x], held.at[a, e]]
@@ -310,60 +371,81 @@
         @pl.when(pos[d] > 0)
         def _(d=d):
             ex_copy(d).wait_send()
+    for copy in stores:
+        copy.wait()
 
 
 def sems(levels):
-    shape = (2, levels + 1, 2)
+    shape = (2, levels + 1, 3)
     return [pltpu.SemaphoreType.DMA(shape)] * 4 + [pltpu.SemaphoreType.DMA((2,))] * 2
 
 
-def gather_rows(tok, cot, levels, lines):
-    if not by_kernel(tok.shape, levels, lines):
-        return tuple(lax.all_gather(v, ("expert", "dp"), axis=0, tiled=True) for v in (tok, cot))
-    full = jax.ShapeDtypeStruct((levels, lines) + tok.shape, tok.dtype)
-    got = pl.pallas_call(
-        functools.partial(gather_kernel, levels),
-        out_shape=(full, full),
-        in_specs=[pl.BlockSpec(memory_space=pl.ANY)] * 2,
-        out_specs=(pl.BlockSpec(memory_space=pl.ANY),) * 2,
-        scratch_shapes=[pltpu.SemaphoreType.DMA((2,))] + sems(levels),
-        compiler_params=pltpu.CompilerParams(collective_id=0, has_side_effects=True),
-    )(tok, cot)
-    return tuple(v.reshape(-1, tok.shape[1]) for v in got)
-
-
-def scatter_sums(y_part, dx_part, levels, lines):
-    width = y_part.shape[1]
+def gather_rows(arrays, levels, lines):
+    if not by_kernel(arrays[0].shape, levels, lines):
+        got = tuple(lax.all_gather(v, ("expert", "dp"), axis=0) for v in arrays)
+    else:
+        anywhere = pl.BlockSpec(memory_space=pl.ANY)
+        got = pl.pallas_call(
+            functools.partial(gather_kernel, levels),
+            out_shape=tuple(jax.ShapeDtypeStruct((levels, lines) + v.shape, v.dtype) for v in arrays),
+            in_specs=[anywhere] * 3,
+            out_specs=(anywhere,) * 3,
+            scratch_shapes=[pltpu.SemaphoreType.DMA((3,))] + sems(levels),
+            compiler_params=pltpu.CompilerParams(collective_id=0, has_side_effects=True),
+        )(*arrays)
+    return tuple(v.reshape((-1,) + a.shape) for v, a in zip(got, arrays))
+
+
+def scatter_sums(y_part, dx_part, gate_delta, up_delta, hidden_w, tok, cot, levels, lines):
+    width, units = y_part.shape[1], hidden_w.shape[1]
     rows = y_part.shape[0] // (levels * lines)
+    low = y_part.dtype
     if not by_kernel((rows, width), levels, lines):
-        return tuple(
+        sums = tuple(
             lax.psum_scatter(v, ("expert", "dp"), scatter_dimension=0, tiled=True) for v in (y_part, dx_part)
         )
-    one = jax.ShapeDtypeStruct((rows, width), y_part.dtype)
+        pairs = ((tok, gate_delta), (tok, up_delta), (hidden_w, cot))
+        return sums + tuple(contract_first(left, right).astype(low) for left, right in pairs)
+    one = jax.ShapeDtypeStruct((rows, width), low)
+    tall, wide = (width, units), (units, width)
     vmem = pl.BlockSpec(memory_space=pltpu.VMEM)
+    anywhere = pl.BlockSpec(memory_space=pl.ANY)
     return pl.pallas_call(
         functools.partial(scatter_kernel, levels),
-        out_shape=(one, one),
-        in_specs=[vmem] * 2,
-        out_specs=(vmem,) * 2,
+        out_shape=(one, one) + tuple(jax.ShapeDtypeStruct(v, low) for v in (tall, tall, wide)),
+        in_specs=[vmem] * 5 + [anywhere] * 2,
+        out_specs=(vmem,) * 2 + (anywhere,) * 3,
         scratch_shapes=[
-            pltpu.VMEM((2, levels, rows, width), y_part.dtype),
-            pltpu.VMEM((2, 2, levels, rows, width), y_part.dtype),
-            pltpu.VMEM((4, rows, width), y_part.dtype),
+            pltpu.VMEM((2, levels, rows, width), low),
+            pltpu.VMEM((2, 2, levels, rows, width), low),
+            pltpu.VMEM((4, rows, width), low),
+            pltpu.VMEM(tok.shape, low),
+            pltpu.VMEM(cot.shape, low),
+            pltpu.VMEM(tall, low),
+            pltpu.VMEM(tall, low),
+            pltpu.VMEM(wide, low),
+            pltpu.SemaphoreType.DMA((2,)),
+            pltpu.SemaphoreType.DMA((3,)),
         ]
         + sems(levels),
         compiler_params=pltpu.CompilerParams(
             collective_id=1, has_side_effects=True, vmem_limit_bytes=VMEM_BYTES
         ),
     )(
-        y_part.reshape(levels, lines, rows, width), dx_part.reshape(levels, lines, rows, width)
+        y_part.reshape(levels, lines, rows, width),
+        dx_part.reshape(levels, lines, rows, width),
+        gate_delta,
+        up_delta,
+        hidden_w,
+        tok,
+        cot,
     )
 
 
 def by_kernel(block, levels, lines):
     rows, width = block
-    blocks = 2 * levels * lines + 6 * levels + 6
-    return lines == 2 and levels > 2 and rows % CHUNK == 0 and 2 * blocks * rows * width < VMEM_BYTES
+    blocks = 4 * levels * lines + 6 * levels + 14
+    return lines == 2 and levels > 2 and rows % CHUNK == 0 and width % TILE == 0 and 2 * blocks * rows * width < VMEM_BYTES
 
 
 def shards(
@@ -381,11 +463,13 @@
     axes = ("expert", "dp")
     me = lax.axis_index("expert")
     levels, lines = lax.axis_size("expert"), lax.axis_size("dp")
-    tok, cot = gather_rows(tokens[0], cotangent[0], levels, lines)
-    ids = lax.all_gather(routes[0].T, axes, axis=1, tiled=True)
-    wts = lax.all_gather(route_weight[0].T, axes, axis=1, tiled=True)
-    hit = ids == me
-    weight = jnp.sum(jnp.where(hit, wts, 0.0), axis=0)[:, None]
+    meta = jnp.concatenate([routes[0].T.astype(jnp.float32), route_weight[0].T], axis=0)
+    meta = jnp.pad(meta, ((0, -meta.shape[0] % 8), (0, 0)))
+    tok, cot, meta = gather_rows((tokens[0], cotangent[0], meta), levels, lines)
+    tok, cot = tok.reshape(-1, tok.shape[-1]), cot.reshape(-1, cot.shape[-1])
+    per_token = routes.shape[-1]
+    hit = meta[:, :per_token] == me.astype(jnp.float32)
+    weight = jnp.sum(jnp.where(hit, meta[:, per_token : 2 * per_token], 0.0), axis=1).reshape(-1, 1)
     gate_w = gate_weight[0, 0]
     up_w = up_weight[0, 0]
     down_w = down_weight[0, 0]
@@ -404,13 +488,12 @@
     gate_delta = (back_w * up_pre * (sig * (1.0 + gate_pre * (1.0 - sig)))).astype(jnp.bfloat16)
     up_delta = (back_w * silu_gate).astype(jnp.bfloat16)
     dx_part = (contract_last(gate_delta, gate_w) + contract_last(up_delta, up_w)).astype(jnp.bfloat16)
-    layer_out, token_grad = scatter_sums(y_part, dx_part, levels, lines)
-    mix_part = jnp.where(hit, mix_rows[None, :], 0.0)
+    layer_out, token_grad, gate_grad, up_grad, down_grad = scatter_sums(
+        y_part, dx_part, gate_delta, up_delta, hidden_w, tok, cot, levels, lines
+    )
+    mix_part = jnp.where(hit, mix_rows.reshape(hit.shape[0], 1, -1), 0.0)
+    mix_part = mix_part.transpose(1, 0, 2).reshape(per_token, -1)
     mix_grad = lax.psum_scatter(mix_part, axes, scatter_dimension=1, tiled=True).T
-
-    gate_grad = contract_first(tok, gate_delta).astype(jnp.bfloat16)
-    up_grad = contract_first(tok, up_delta).astype(jnp.bfloat16)
-    down_grad = contract_first(hidden_w, cot).astype(jnp.bfloat16)
 
     island_count = lax.axis_size("replica")
     summed = lax.psum_scatter(

time: 342 us -> 312 us (0.912)
  blocking collectives: 39.3 us -> 0 us
  Pallas kernels: 237 us -> 255 us
  matrix products: 39.9 us -> 25 us
  local copies, waits for them, and re-layouts: 4.76 us -> 10.1 us
    all_gather x2 -> x0, blocking collectives: 39.3 us -> none  [the longest x1 22.6 us: shards(): ids = lax.all_gather(routes[0].T, axes, axis=1, tiled=True)]
    dot_general x3 -> x0, matrix products: 17.5 us -> none  [contract_first(): lax.dot_general(left, right, (((0,), (0,)), ((), ())), preferred_element_...]
    pallas_call x1, Pallas kernels: 114 us -> 125 us  [gather_rows(): pl.pallas_call(functools.partial(gather_kernel, levels), out_shape=tuple(...]
    pallas_call x1, Pallas kernels: 122 us -> 130 us  [scatter_sums(): pl.pallas_call(functools.partial(scatter_kernel, levels), out_shape=(one,...]
    unnamed x30 -> x43, local copies, waits for them, and re-layouts: 4.76 us -> 10.1 us
  transfers between devices with their start and end apart: 2 -> 2, of which waited for: 0 -> 0; matrix products, arithmetic and copies ran while one was open for 10% -> 5% of each run, Pallas kernels for 36% -> 42%
where the time goes in v2:
time: 312 us
  Pallas kernels  255 us (82%)
  matrix products  25 us (8%)
  between operations  14.2 us (5%)
  local copies, waits for them, and re-layouts  10.1 us (3%)
  other arithmetic  7.84 us (3%)
    pallas_call x1, Pallas kernels, scatter_sums(): pl.pallas_call(functools.partial(scatter_kernel, levels), out_shape=(one,...  130 us
    pallas_call x1, Pallas kernels, gather_rows(): pl.pallas_call(functools.partial(gather_kernel, levels), out_shape=tuple(...  125 us
    dot_general x3, matrix products, contract_last(): lax.dot_general(left, right, (((1,), (1,)), ((), ())), preferred_element_...  12.1 us
    unnamed x43, local copies, waits for them, and re-layouts  10.1 us
  transfers between devices with their start and end apart: 2, of which 0 were waited for; matrix products, arithmetic and copies ran while one was open for 5% of the time, Pallas kernels for 42%

profile of v2, /device:TPU:0, one launch (start us, length us, event | category | flops | bytes accessed | tf_op | source)
XLA Modules:
  0.0 312.1 jit_solution(16676887796051697478)
XLA Ops:
  7.2 0.0 copy-start
  7.2 0.0 copy-start.8
  7.2 0.0 reduce-scatter.7.cloned.1.call-start
  7.2 0.8 convert_bitcast_fusion.1
  8.1 1.3 select_maximum_fusion.meta
  9.4 124.9 %shard_map.161 = (bf16[4,2,128,3072]{3,2,1,0:T(8,128)(2,1)}, bf16[4,2,128,3072]{3,2,1,0:T(8,128)(2,1)}, f32[4,2,8,128]{3,2,1,0:T(8,128)}) custom-call(bf16[128,3072]{1,0:T(8,128)(2,1)} %bitcast.80, bf16[128,3072]{1,0:T(8,128)(2,1)} %bitcast.81, f32[8,128]{1,0:T(8,128)} %select_maximum_fusion.meta), custom_call_target="tpu_custom_call" | custom-call | tf_op jit(solution)/shard_map/pallas_call | solution.py:388
  134.3 0.0 copy-done.8
  134.3 0.0 copy-start.2
  134.3 0.0 copy-start.6
  134.3 5.7 %fusion.4 = f32[1024,256]{1,0:T(8,128)} fusion(bf16[1024,3072]{1,0:T(8,128)(2,1)} %bitcast.71, bf16[1,1,3072,256]{3,2,1,0:T(8,128)(2,1)S(1)} %copy-done.8), kind=kOutput, calls=%fused_computation.6 | convolution fusion | flops 1610612736 | bytes 8912896 | tf_op jit(solution)/shard_map/dot_general | solution.py:478
  140.0 0.0 copy-done.2
  140.0 0.0 copy-done.6
  140.0 2.8 fusion.8
  142.8 0.0 copy-done.17
  142.8 0.0 copy-done
  142.8 5.7 %multiply_reduce_fusion = (f32[1024]{0:T(1024)S(1)}, bf16[1024,256]{1,0:T(8,128)(2,1)S(1)}, bf16[1024,256]{1,0:T(8,128)(2,1)S(1)}, bf16[1024,256]{1,0:T(8,128)(2,1)S(1)}) fusion(f32[1024,256]{1,0:T(8,128)} %fusion.4, f32[1024,256]{1,0:T(8,128)} %fusion.8, f32[1024]{0:T(1024)S(1)} %bitcast.88, bf16[1024,3072]{1,0:T(8,128)(2,1)} %bitcast.74, ...), kind=kOutput, calls=%fused_computation.13 | convolution fusion | flops 1615592448 | bytes 11542528 | tf_op jit(solution)/shard_map/dot_general | solution.py:15
  148.5 0.0 copy-start.3
  148.5 0.0 copy-start.4
  148.5 0.0 copy-start.5
  148.5 1.2 copy.35
  149.7 0.0 reduce-scatter.7.cloned.1.call-update
  149.7 0.0 reduce-scatter.5.cloned.1.call-start
  149.8 3.3 %convert_bitcast_fusion = bf16[256,3072]{1,0:T(8,128)(2,1)} fusion(f32[1,1,256,3072]{3,2,1,0:T(8,128)} %param.17), kind=kLoop, calls=%fused_computation.12 | loop fusion | flops 786432 | bytes 4718592 | tf_op jit(solution)/shard_map/convert_element_type | solution.py:500
  153.0 0.0 reduce-scatter.5.cloned.1.call-update
  153.1 0.0 copy-done.3
  153.1 0.0 copy-start.7
  153.1 4.4 %convolution_convert_fusion = bf16[1024,3072]{1,0:T(8,128)(2,1)} fusion(bf16[1024,256]{1,0:T(8,128)(2,1)S(1)} %get-tuple-element.26.hidden_w, bf16[1,1,256,3072]{3,2,1,0:T(8,128)(2,1)S(1)} %copy-done), kind=kOutput, calls=%fused_computation.1 | convolution fusion | flops 1613758464 | bytes 8388608 | tf_op jit(solution)/shard_map/dot_general | solution.py:483
  157.5 0.0 copy-done.4
  157.5 0.0 copy-done.7
  157.5 1.8 fusion.6
  159.3 0.0 copy-done.5
  159.3 0.0 copy-done.9
  159.4 4.6 %add_convert_fusion = bf16[1024,3072]{1,0:T(8,128)(2,1)} fusion(f32[1024,3072]{1,0:T(8,128)S(1)} %fusion.6, bf16[1024,256]{1,0:T(8,128)(2,1)S(1)} %get-tuple-element.27.up_delta, bf16[1,1,3072,256]{3,2,1,0:T(8,128)(2,1)S(1)} %copy-done.9), kind=kOutput, calls=%fused_computation | convolution fusion | flops 1616904192 | bytes 20971520 | tf_op jit(solution)/shard_map/dot_general | solution.py:15
  164.0 130.0 %shard_map.162 = (bf16[128,3072]{1,0:T(8,128)(2,1)}, bf16[128,3072]{1,0:T(8,128)(2,1)}, bf16[3072,256]{1,0:T(8,128)(2,1)}, bf16[3072,256]{1,0:T(8,128)(2,1)}, bf16[256,3072]{1,0:T(8,128)(2,1)}) custom-call(bf16[4,2,128,3072]{3,2,1,0:T(8,128)(2,1)} %bitcast.69, bf16[4,2,128,3072]{3,2,1,0:T(8,128)(2,1)} %bitcast.70, bf16[1024,256]{1,0:T(8,128)(2,1)} %copy-done.4, ...), custom_call_target="tpu_custom_call" | custom-call | tf_op jit(solution)/shard_map/pallas_call | solution.py:413
  294.0 0.0 reduce-scatter.7.cloned.1.call-done
  294.0 1.5 copy.36
  295.5 0.0 copy-done.13
  295.5 0.0 copy-done.14
  295.5 2.4 fusion.12
  297.9 0.0 copy-done.16
  297.9 0.9 copy.42
  298.8 0.5 copy-done.15
  299.3 0.9 copy.43
  300.2 1.1 copy.44
  301.3 0.8 copy-done.11
  302.2 1.1 copy.45
  303.3 0.8 copy-done.10
  304.2 1.1 copy.46
  (15 shorter events, 0.1 us)
Async XLA Ops:
  7.2 135.6 %copy-start = (bf16[1,1,256,3072]{3,2,1,0:T(8,128)(2,1)S(1)}, bf16[1,1,256,3072]{3,2,1,0:T(8,128)(2,1)}, u32[]{:S(2)}) copy-start(bf16[1,1,256,3072]{3,2,1,0:T(8,128)(2,1)} %param.16) | copy-start | bytes 4718596
  7.2 127.1 %copy-start.8 = (bf16[1,1,3072,256]{3,2,1,0:T(8,128)(2,1)S(1)}, bf16[1,1,3072,256]{3,2,1,0:T(8,128)(2,1)}, u32[]{:S(2)}) copy-start(bf16[1,1,3072,256]{3,2,1,0:T(8,128)(2,1)} %param.15) | copy-start | bytes 4718596
  7.2 286.8 %reduce-scatter.7.cloned.1.call-start = ((), (), s32[]{:S(2)}) async-start(), calls=%async_computation.3 | async-start | bytes 589824
  134.3 5.7 %copy-start.2 = (bf16[4,2,128,3072]{3,2,1,0:T(8,128)(2,1)S(1)}, bf16[4,2,128,3072]{3,2,1,0:T(8,128)(2,1)}, u32[]{:S(2)}) copy-start(bf16[4,2,128,3072]{3,2,1,0:T(8,128)(2,1)} %get-tuple-element.16) | copy-start | bytes 18874372
  134.3 5.7 %copy-start.6 = (bf16[1,1,3072,256]{3,2,1,0:T(8,128)(2,1)S(1)}, bf16[1,1,3072,256]{3,2,1,0:T(8,128)(2,1)}, u32[]{:S(2)}) copy-start(bf16[1,1,3072,256]{3,2,1,0:T(8,128)(2,1)} %param.14) | copy-start | bytes 4718596
  140.0 2.8 copy-start.17
  148.5 4.6 %copy-start.3 = (bf16[1024,256]{1,0:T(8,128)(2,1)}, bf16[1024,256]{1,0:T(8,128)(2,1)S(1)}, u32[]{:S(2)}) copy-start(bf16[1024,256]{1,0:T(8,128)(2,1)S(1)} %get-tuple-element.26.hidden_w) | copy-start | bytes 1572868
  148.5 9.0 %copy-start.4 = (bf16[1024,256]{1,0:T(8,128)(2,1)}, bf16[1024,256]{1,0:T(8,128)(2,1)S(1)}, u32[]{:S(2)}) copy-start(bf16[1024,256]{1,0:T(8,128)(2,1)S(1)} %get-tuple-element.25.gate_delta) | copy-start | bytes 1572868
  148.5 10.9 %copy-start.5 = (bf16[1024,256]{1,0:T(8,128)(2,1)}, bf16[1024,256]{1,0:T(8,128)(2,1)S(1)}, u32[]{:S(2)}) copy-start(bf16[1024,256]{1,0:T(8,128)(2,1)S(1)} %get-tuple-element.27.up_delta) | copy-start | bytes 1572868
  149.7 145.7 %reduce-scatter.5.cloned.1.call-start = ((), (), s32[]{:S(2)}) async-start(), calls=%async_computation.2 | async-start | bytes 1966080 | tf_op jit(solution)/shard_map/reduce_scatter | solution.py:499
  153.1 4.4 %copy-start.7 = (bf16[1,1,3072,256]{3,2,1,0:T(8,128)(2,1)S(1)}, bf16[1,1,3072,256]{3,2,1,0:T(8,128)(2,1)}, u32[]{:S(2)}) copy-start(bf16[1,1,3072,256]{3,2,1,0:T(8,128)(2,1)} %param.14) | copy-start | bytes 4718596
  157.5 1.9 copy-start.9
  164.0 131.5 %copy-start.13 = (f32[1,256,768]{2,1,0:T(8,128)S(1)}, f32[1,256,768]{2,1,0:T(8,128)}, u32[]{:S(2)}) copy-start(f32[1,256,768]{2,1,0:T(8,128)} %param.19) | copy-start | bytes 2359300
  164.0 131.5 %copy-start.14 = (f32[1,256,768]{2,1,0:T(8,128)S(1)}, f32[1,256,768]{2,1,0:T(8,128)}, u32[]{:S(2)}) copy-start(f32[1,256,768]{2,1,0:T(8,128)} %param.18) | copy-start | bytes 2359300
  295.5 2.4 copy-start.16
  297.9 1.4 copy-start.15
  297.9 2.3 copy-start.12
  300.2 2.0 copy-start.11
  302.2 2.0 copy-start.10
  302.2 3.1 copy-start.1
Sparse Core Ops, SparseCore 0:
  149.9 63.1 reduce-scatter.6
  216.3 27.2 reduce-scatter.4

commit v3 on v2

--- a/solution.py
+++ b/solution.py
@@ -59,13 +59,16 @@
     )
 
 
-def gather_kernel(levels, tok, cot, meta, tok_all, cot_all, meta_all, own_sem, z_send, z_recv, x_send, x_recv, ex_send, ex_recv):
+def gather_kernel(
+    levels, tok, cot, meta, outer, tok_all, cot_all, meta_all, outer_low, outer_in, outer_sem, own_sem, z_send, z_recv, x_send, x_recv, ex_send, ex_recv):
     e, x = lax.axis_index("expert"), lax.axis_index("dp")
     last = levels - 1
     mine, full = (tok, cot, meta), (tok_all, cot_all, meta_all)
     order = (2, 0, 1)
     pos = (e, last - e)
     sign = (-1, 1)
+    load = pltpu.make_async_copy(outer, outer_in, outer_sem)
+    load.start()
     enter(levels)
     local = [pltpu.make_async_copy(mine[a], full[a].at[e, x], own_sem.at[a]) for a in order]
     for copy in local:
@@ -103,6 +106,15 @@
             @pl.when(pos[d] < last)
             def _(d=d, a=a):
                 z_copy(d, 1, a).start()
+
+    load.wait()
+
+    def narrow(i, carry):
+        at = pl.ds(pl.multiple_of(i * CHUNK, CHUNK), CHUNK)
+        outer_low[at, :] = outer_in[at, :].astype(outer_low.dtype)
+        return carry
+
+    lax.fori_loop(0, outer_in.shape[0] // CHUNK, narrow, 0)
 
     for k in range(1, levels):
         for a in order:
@@ -380,20 +392,27 @@
     return [pltpu.SemaphoreType.DMA(shape)] * 4 + [pltpu.SemaphoreType.DMA((2,))] * 2
 
 
-def gather_rows(arrays, levels, lines):
+def gather_rows(arrays, outer, levels, lines):
     if not by_kernel(arrays[0].shape, levels, lines):
         got = tuple(lax.all_gather(v, ("expert", "dp"), axis=0) for v in arrays)
+        low = outer.astype(jnp.bfloat16)
     else:
         anywhere = pl.BlockSpec(memory_space=pl.ANY)
-        got = pl.pallas_call(
+        *got, low = pl.pallas_call(
             functools.partial(gather_kernel, levels),
-            out_shape=tuple(jax.ShapeDtypeStruct((levels, lines) + v.shape, v.dtype) for v in arrays),
-            in_specs=[anywhere] * 3,
-            out_specs=(anywhere,) * 3,
-            scratch_shapes=[pltpu.SemaphoreType.DMA((3,))] + sems(levels),
-            compiler_params=pltpu.CompilerParams(collective_id=0, has_side_effects=True),
-        )(*arrays)
-    return tuple(v.reshape((-1,) + a.shape) for v, a in zip(got, arrays))
+            out_shape=tuple(jax.ShapeDtypeStruct((levels, lines) + v.shape, v.dtype) for v in arrays)
+            + (jax.ShapeDtypeStruct(outer.shape, jnp.bfloat16),),
+            in_specs=[anywhere] * 4,
+            out_specs=(anywhere,) * 3 + (pl.BlockSpec(memory_space=pltpu.VMEM),),
+            scratch_shapes=[
+                pltpu.VMEM(outer.shape, outer.dtype),
+                pltpu.SemaphoreType.DMA,
+                pltpu.SemaphoreType.DMA((3,)),
+            ]
+            + sems(levels),
+            compiler_params=pltpu.CompilerParams(collective_id=0, has_side_effects=True, vmem_limit_bytes=VMEM_BYTES),
+        )(*arrays, outer)
+    return tuple(v.reshape((-1,) + a.shape) for v, a in zip(got, arrays)) + (low,)
 
 
 def scatter_sums(y_part, dx_part, gate_delta, up_delta, hidden_w, tok, cot, levels, lines):
@@ -465,7 +484,9 @@
     levels, lines = lax.axis_size("expert"), lax.axis_size("dp")
     meta = jnp.concatenate([routes[0].T.astype(jnp.float32), route_weight[0].T], axis=0)
     meta = jnp.pad(meta, ((0, -meta.shape[0] % 8), (0, 0)))
-    tok, cot, meta = gather_rows((tokens[0], cotangent[0], meta), levels, lines)
+    tok, cot, meta, outer_low = gather_rows(
+        (tokens[0], cotangent[0], meta), pseudo_grad[0, 0], levels, lines
+    )
     tok, cot = tok.reshape(-1, tok.shape[-1]), cot.reshape(-1, cot.shape[-1])
     per_token = routes.shape[-1]
     hit = meta[:, :per_token] == me.astype(jnp.float32)
@@ -497,7 +518,7 @@
 
     island_count = lax.axis_size("replica")
     summed = lax.psum_scatter(
-        pseudo_grad[0, 0].astype(jnp.bfloat16), "replica", scatter_dimension=1, tiled=True
+        outer_low, "replica", scatter_dimension=1, tiled=True
     ).astype(jnp.float32)
     mean_grad = summed / island_count
     new_momentum = OUTER_MU * momentum[0] + mean_grad

time: 312 us -> 311 us (level)
  other arithmetic: 7.84 us -> 4.51 us
    convert_element_type x1 -> x0, other arithmetic: 3.25 us -> none  [shards(): pseudo_grad[0, 0].astype(jnp.bfloat16)]
  transfers between devices with their start and end apart: 2 -> 2, of which waited for: 0 -> 0; matrix products, arithmetic and copies ran while one was open for 5% -> 4% of each run, Pallas kernels for 42% -> 42%
where the time goes in v3:
time: 311 us
  Pallas kernels  256 us (82%)
  matrix products  24.9 us (8%)
  between operations  14.2 us (5%)
  local copies, waits for them, and re-layouts  10.2 us (3%)
  other arithmetic  4.51 us (1%)
    pallas_call x1, Pallas kernels, scatter_sums(): pl.pallas_call(functools.partial(scatter_kernel, levels), out_shape=(one,...  130 us
    pallas_call x1, Pallas kernels, gather_rows(): pl.pallas_call(functools.partial(gather_kernel, levels), out_shape=tuple(...  126 us
    dot_general x3, matrix products, contract_last(): lax.dot_general(left, right, (((1,), (1,)), ((), ())), preferred_element_...  12.1 us
    unnamed x43, local copies, waits for them, and re-layouts  10.2 us
  transfers between devices with their start and end apart: 2, of which 0 were waited for; matrix products, arithmetic and copies ran while one was open for 4% of the time, Pallas kernels for 42%

profile of v3, /device:TPU:0, one launch (start us, length us, event | category | flops | bytes accessed | tf_op | source)
XLA Modules:
  0.0 311.0 jit_solution(11627246790246768515)
XLA Ops:
  7.2 0.0 copy-start
  7.2 0.0 reduce-scatter.7.cloned.1.call-start
  7.2 0.8 convert_bitcast_fusion
  8.0 1.3 select_maximum_fusion.meta
  9.3 126.1 %shard_map.161 = (bf16[4,2,128,3072]{3,2,1,0:T(8,128)(2,1)}, bf16[4,2,128,3072]{3,2,1,0:T(8,128)(2,1)}, f32[4,2,8,128]{3,2,1,0:T(8,128)}, bf16[256,3072]{1,0:T(8,128)(2,1)}) custom-call(bf16[128,3072]{1,0:T(8,128)(2,1)} %bitcast.82, bf16[128,3072]{1,0:T(8,128)(2,1)} %bitcast.83, f32[8,128]{1,0:T(8,128)} %select_maximum_fusion.meta, f32[256,3072]{1,0:T(8,128)} %bitcast.75), custom_call_target="tpu_custom_call" | custom-call | tf_op jit(solution)/shard_map/pallas_call | solution.py:401
  135.4 0.0 copy-done.8
  135.4 0.0 copy-start.2
  135.4 0.0 copy-start.6
  135.4 5.7 %fusion.4 = f32[1024,256]{1,0:T(8,128)} fusion(bf16[1024,3072]{1,0:T(8,128)(2,1)} %bitcast.70, bf16[1,1,3072,256]{3,2,1,0:T(8,128)(2,1)S(1)} %copy-done.8), kind=kOutput, calls=%fused_computation.6 | convolution fusion | flops 1610612736 | bytes 8912896 | tf_op jit(solution)/shard_map/dot_general | solution.py:499
  141.1 0.0 copy-done.2
  141.1 0.0 copy-done.6
  141.1 2.8 fusion.8
  143.9 0.0 copy-done.17
  143.9 0.0 copy-done
  143.9 5.6 %multiply_reduce_fusion = (f32[1024]{0:T(1024)S(1)}, bf16[1024,256]{1,0:T(8,128)(2,1)S(1)}, bf16[1024,256]{1,0:T(8,128)(2,1)S(1)}, bf16[1024,256]{1,0:T(8,128)(2,1)S(1)}) fusion(f32[1024,256]{1,0:T(8,128)} %fusion.4, f32[1024,256]{1,0:T(8,128)} %fusion.8, f32[1024]{0:T(1024)S(1)} %bitcast.88, bf16[1024,3072]{1,0:T(8,128)(2,1)} %bitcast.73, ...), kind=kOutput, calls=%fused_computation.12 | convolution fusion | flops 1615592448 | bytes 11542528 | tf_op jit(solution)/shard_map/dot_general | solution.py:15
  149.6 0.0 copy-start.3
  149.6 0.0 copy-start.4
  149.6 0.0 copy-start.5
  149.6 1.3 copy.35
  150.9 0.0 reduce-scatter.7.cloned.1.call-update
  150.9 0.0 reduce-scatter.5.cloned.1.call-start
  151.0 0.7 reduce-scatter.5.cloned.1.call-update
  151.7 0.0 copy-start.7
  151.7 4.4 %convolution_convert_fusion = bf16[1024,3072]{1,0:T(8,128)(2,1)} fusion(bf16[1024,256]{1,0:T(8,128)(2,1)S(1)} %get-tuple-element.28.hidden_w, bf16[1,1,256,3072]{3,2,1,0:T(8,128)(2,1)S(1)} %copy-done), kind=kOutput, calls=%fused_computation.1 | convolution fusion | flops 1613758464 | bytes 8388608 | tf_op jit(solution)/shard_map/dot_general | solution.py:504
  156.1 0.0 copy-done.3
  156.1 0.0 copy-done.4
  156.1 0.0 copy-done.7
  156.1 1.8 fusion.6
  158.0 0.0 copy-done.5
  158.0 0.0 copy-done.9
  158.0 4.6 %add_convert_fusion = bf16[1024,3072]{1,0:T(8,128)(2,1)} fusion(f32[1024,3072]{1,0:T(8,128)S(1)} %fusion.6, bf16[1024,256]{1,0:T(8,128)(2,1)S(1)} %get-tuple-element.29.up_delta, bf16[1,1,3072,256]{3,2,1,0:T(8,128)(2,1)S(1)} %copy-done.9), kind=kOutput, calls=%fused_computation | convolution fusion | flops 1616904192 | bytes 20971520 | tf_op jit(solution)/shard_map/dot_general | solution.py:15
  162.6 130.2 %shard_map.162 = (bf16[128,3072]{1,0:T(8,128)(2,1)}, bf16[128,3072]{1,0:T(8,128)(2,1)}, bf16[3072,256]{1,0:T(8,128)(2,1)}, bf16[3072,256]{1,0:T(8,128)(2,1)}, bf16[256,3072]{1,0:T(8,128)(2,1)}) custom-call(bf16[4,2,128,3072]{3,2,1,0:T(8,128)(2,1)} %bitcast.68, bf16[4,2,128,3072]{3,2,1,0:T(8,128)(2,1)} %bitcast.69, bf16[1024,256]{1,0:T(8,128)(2,1)} %copy-done.4, ...), custom_call_target="tpu_custom_call" | custom-call | tf_op jit(solution)/shard_map/pallas_call | solution.py:432
  292.8 0.0 reduce-scatter.7.cloned.1.call-done
  292.9 1.5 copy.36
  294.3 0.0 copy-done.13
  294.3 0.0 copy-done.14
  294.3 2.4 fusion.12
  296.8 0.0 copy-done.16
  296.8 0.9 copy.42
  297.6 0.5 copy-done.15
  298.2 0.9 copy.43
  299.1 0.0 copy-done.12
  299.1 1.1 copy.44
  300.2 0.8 copy-done.11
  301.0 1.1 copy.45
  302.2 0.8 copy-done.10
  303.0 1.1 copy.46
  304.2 0.0 copy-done.1
  (14 shorter events, 0.0 us)
Async XLA Ops:
  7.2 136.8 %copy-start = (bf16[1,1,256,3072]{3,2,1,0:T(8,128)(2,1)S(1)}, bf16[1,1,256,3072]{3,2,1,0:T(8,128)(2,1)}, u32[]{:S(2)}) copy-start(bf16[1,1,256,3072]{3,2,1,0:T(8,128)(2,1)} %param.16) | copy-start | bytes 4718596
  7.2 285.7 %reduce-scatter.7.cloned.1.call-start = ((), (), s32[]{:S(2)}) async-start(), calls=%async_computation.3 | async-start | bytes 589824
  9.3 126.1 %copy-start.8 = (bf16[1,1,3072,256]{3,2,1,0:T(8,128)(2,1)S(1)}, bf16[1,1,3072,256]{3,2,1,0:T(8,128)(2,1)}, u32[]{:S(2)}) copy-start(bf16[1,1,3072,256]{3,2,1,0:T(8,128)(2,1)} %param.15) | copy-start | bytes 4718596
  135.4 5.7 %copy-start.2 = (bf16[4,2,128,3072]{3,2,1,0:T(8,128)(2,1)S(1)}, bf16[4,2,128,3072]{3,2,1,0:T(8,128)(2,1)}, u32[]{:S(2)}) copy-start(bf16[4,2,128,3072]{3,2,1,0:T(8,128)(2,1)} %get-tuple-element.17) | copy-start | bytes 18874372
  135.4 5.7 %copy-start.6 = (bf16[1,1,3072,256]{3,2,1,0:T(8,128)(2,1)S(1)}, bf16[1,1,3072,256]{3,2,1,0:T(8,128)(2,1)}, u32[]{:S(2)}) copy-start(bf16[1,1,3072,256]{3,2,1,0:T(8,128)(2,1)} %param.14) | copy-start | bytes 4718596
  141.1 2.8 copy-start.17
  149.6 6.5 %copy-start.3 = (bf16[1024,256]{1,0:T(8,128)(2,1)}, bf16[1024,256]{1,0:T(8,128)(2,1)S(1)}, u32[]{:S(2)}) copy-start(bf16[1024,256]{1,0:T(8,128)(2,1)S(1)} %get-tuple-element.28.hidden_w) | copy-start | bytes 1572868
  149.6 6.5 %copy-start.4 = (bf16[1024,256]{1,0:T(8,128)(2,1)}, bf16[1024,256]{1,0:T(8,128)(2,1)S(1)}, u32[]{:S(2)}) copy-start(bf16[1024,256]{1,0:T(8,128)(2,1)S(1)} %get-tuple-element.27.gate_delta) | copy-start | bytes 1572868
  149.6 8.4 %copy-start.5 = (bf16[1024,256]{1,0:T(8,128)(2,1)}, bf16[1024,256]{1,0:T(8,128)(2,1)S(1)}, u32[]{:S(2)}) copy-start(bf16[1024,256]{1,0:T(8,128)(2,1)S(1)} %get-tuple-element.29.up_delta) | copy-start | bytes 1572868
  150.9 143.4 %reduce-scatter.5.cloned.1.call-start = ((), (), s32[]{:S(2)}) async-start(), calls=%async_computation.2 | async-start | bytes 1966080 | tf_op jit(solution)/shard_map/reduce_scatter | solution.py:520
  151.7 4.4 %copy-start.7 = (bf16[1,1,3072,256]{3,2,1,0:T(8,128)(2,1)S(1)}, bf16[1,1,3072,256]{3,2,1,0:T(8,128)(2,1)}, u32[]{:S(2)}) copy-start(bf16[1,1,3072,256]{3,2,1,0:T(8,128)(2,1)} %param.14) | copy-start | bytes 4718596
  156.1 1.9 copy-start.9
  162.6 131.8 %copy-start.13 = (f32[1,256,768]{2,1,0:T(8,128)S(1)}, f32[1,256,768]{2,1,0:T(8,128)}, u32[]{:S(2)}) copy-start(f32[1,256,768]{2,1,0:T(8,128)} %param.19) | copy-start | bytes 2359300
  162.6 131.8 %copy-start.14 = (f32[1,256,768]{2,1,0:T(8,128)S(1)}, f32[1,256,768]{2,1,0:T(8,128)}, u32[]{:S(2)}) copy-start(f32[1,256,768]{2,1,0:T(8,128)} %param.18) | copy-start | bytes 2359300
  294.3 2.4 copy-start.16
  296.8 1.4 copy-start.15
  296.8 2.3 copy-start.12
  299.1 2.0 copy-start.11
  301.0 2.0 copy-start.10
  301.0 3.1 %copy-start.1 = (bf16[1,1,256,3072]{3,2,1,0:T(8,128)(2,1)S(1)}, bf16[1,1,256,3072]{3,2,1,0:T(8,128)(2,1)}, u32[]{:S(2)}) copy-start(bf16[1,1,256,3072]{3,2,1,0:T(8,128)(2,1)} %param.16) | copy-start | bytes 4718596
Sparse Core Ops, SparseCore 0:
  151.0 63.2 reduce-scatter.6
  217.1 27.1 reduce-scatter.4
